TPU v7x, 32 devices: a whole 2x2x4 slice. The times are simulated.
32 devices in a mesh: node: 1, ep: 32 (over z, y, x, core).
Axes of the slice: x: 2, y: 2, z: 4, core: 2. Of those that a mesh axis runs over, the one named last changes fastest.
Arguments:
- images: bfloat16 [32, 257, 1280], P(('node', 'ep')), may hold values from -6 to 6
- w_query: bfloat16 [1280, 1280], P(None, 'node'), may hold values from -6 to 6
- w_key: bfloat16 [1280, 1280], P(None, 'node'), may hold values from -6 to 6
- w_value: bfloat16 [1280, 1280], P(None, 'node'), may hold values from -0.15625 to 0.15625
- w_output: bfloat16 [1280, 1280], replicated, may hold values from -0.15625 to 0.15625
- router: bfloat16 [1280, 32], replicated, may hold values from -0.15625 to 0.15625
- w_in: bfloat16 [32, 1280, 5120], P('ep', None, 'node'), may hold values from -0.15625 to 0.15625
- w_out: bfloat16 [32, 5120, 1280], P('ep', 'node'), may hold values from -0.078125 to 0.078125
- routes: int32 [32, 257, 2], P(('node', 'ep')), may hold values from 0 to 31, all different within a row; in each aligned block of 257 rows (0 to 256, 257 to 513, ..., all dimensions but the last counted through in order) at most 24 rows name the same one
Outputs:
- output: bfloat16 [32, 257, 1280], P(('node', 'ep'))
Inputs may be any that keep to these rules, and one draw needn't show every extreme that they name: `routes`: the two experts of a token differ. At most 24 tokens of one image name the same expert, and in every draw some image has an expert named by exactly 24 of its tokens.
All inputs are finite; a program needn't handle non-finite values.
Results may differ from a plain program's by a relative error of at most 0.0085.
Values may be sent and summed in bfloat16 or wider, within the bound.
A program may use at most 128 MiB of HBM per device.

v0:
```python
import math

import jax
import jax.numpy as jnp
from jax import lax
from jax.sharding import PartitionSpec as P

D = 1280
HEADS = 16
CAP = 24


def layer_norm(values):
    center = values - jnp.mean(values, axis=-1, keepdims=True)
    spread = jnp.mean(center * center, axis=-1, keepdims=True)
    return center * lax.rsqrt(spread + 1e-06)


def slot_table(chosen, num_experts):
    onehot = (chosen[..., None] == jnp.arange(num_experts, dtype=jnp.int32)).astype(jnp.int32)
    before = jnp.cumsum(onehot, axis=1) - onehot
    return jnp.sum(before * onehot, axis=-1)


def shards(images, w_query, w_key, w_value, w_output, router, w_in, w_out, routes):
    local_images, tokens_dev, width = images.shape
    head_size = D // HEADS
    local_heads = w_query.shape[1] // head_size
    node_count = lax.axis_size("node")
    column_count = lax.axis_size("ep")
    num_experts = router.shape[1]
    local_experts = w_in.shape[0]
    slot_count = local_images * CAP
    inputs = images.astype(jnp.float32)
    normed = layer_norm(inputs).astype(jnp.bfloat16)
    shard_rows = lax.all_gather(normed, "node", axis=0, tiled=True)
    number = shard_rows.shape[0]
    queries = jnp.einsum(
        "ctd,de->cte", shard_rows, w_query, preferred_element_type=jnp.float32
    ).astype(jnp.bfloat16)
    projected_keys = jnp.einsum(
        "ctd,de->cte", shard_rows, w_key, preferred_element_type=jnp.float32
    ).astype(jnp.bfloat16)
    projected_values = jnp.einsum(
        "ctd,de->cte", shard_rows, w_value, preferred_element_type=jnp.float32
    ).astype(jnp.bfloat16)
    query_heads = queries.reshape(number, tokens_dev, local_heads, head_size)
    key_heads = projected_keys.reshape(number, tokens_dev, local_heads, head_size)
    value_heads = projected_values.reshape(number, tokens_dev, local_heads, head_size)
    scores = jnp.einsum(
        "cqhd,ckhd->chqk", query_heads, key_heads, preferred_element_type=jnp.float32
    ) / math.sqrt(head_size)
    weights = jax.nn.softmax(scores, axis=-1).astype(jnp.bfloat16)
    mixture = jnp.einsum(
        "chqk,ckhd->cqhd", weights, value_heads, preferred_element_type=jnp.float32
    ).astype(jnp.bfloat16)
    head_results = mixture.reshape(number, tokens_dev, local_heads * head_size)
    attention = jnp.einsum(
        "itd,de->ite",
        lax.all_to_all(head_results, "node", split_axis=0, concat_axis=2, tiled=True),
        w_output,
        preferred_element_type=jnp.float32,
    )
    middle = inputs + attention
    normed_second = layer_norm(middle).astype(jnp.bfloat16)
    logits = jnp.einsum("itd,de->ite", normed_second, router, preferred_element_type=jnp.float32)
    chosen_mask = routes[..., None] == jnp.arange(num_experts, dtype=jnp.int32)
    chosen_logit = jnp.sum(jnp.where(chosen_mask, logits[:, :, None, :], jnp.float32(0.0)), axis=-1)
    gate_values = jax.nn.sigmoid(chosen_logit)
    flat_routes = routes.reshape(local_images, 2 * tokens_dev)
    slot_index = slot_table(flat_routes, num_experts)
    image_base = jnp.arange(local_images, dtype=jnp.int32)[:, None] * CAP
    position = (flat_routes * slot_count + image_base + slot_index).reshape(-1)
    token_ids = jnp.arange(local_images * 2 * tokens_dev, dtype=jnp.int32) // 2
    source = jnp.full((num_experts * slot_count,), -1, jnp.int32).at[position].set(token_ids)
    token_rows = normed_second.reshape(local_images * tokens_dev, width)
    gathered = jnp.take(token_rows, jnp.maximum(source, 0), axis=0)
    gathered = jnp.where(source[:, None] >= 0, gathered, jnp.zeros_like(gathered))
    outgoing = gathered.reshape(column_count, local_experts, slot_count, width)
    copies = jnp.broadcast_to(outgoing[None], (node_count,) + outgoing.shape)
    copies = copies.reshape(node_count * column_count, local_experts, slot_count, width)
    arrived = lax.all_to_all(copies, ("node", "ep"), split_axis=0, concat_axis=0, tiled=True)
    pre_act = jnp.einsum("lesd,edf->lesf", arrived, w_in, preferred_element_type=jnp.float32)
    hidden = jax.nn.gelu(pre_act, approximate=True).astype(jnp.bfloat16)
    partial_sum = jnp.einsum(
        "lesf,efd->lesd", hidden, w_out, preferred_element_type=jnp.float32
    ).astype(jnp.bfloat16)
    returned = lax.all_to_all(partial_sum, ("node", "ep"), split_axis=0, concat_axis=0, tiled=True)
    returned = returned.astype(jnp.float32).reshape(
        node_count, column_count, local_experts, slot_count, width
    )
    expert_result = jnp.sum(returned, axis=0).astype(jnp.bfloat16)
    result_rows = expert_result.reshape(num_experts * slot_count, width)
    picked = jnp.take(result_rows, position, axis=0).reshape(local_images, tokens_dev, 2, width)
    expert_mix = jnp.sum(gate_values[..., None] * picked.astype(jnp.float32), axis=2)
    return (middle + expert_mix).astype(jnp.bfloat16)


def solution(mesh):
    placed = (
        P(("node", "ep"), None, None),
        P(None, "node"),
        P(None, "node"),
        P(None, "node"),
        P(),
        P(),
        P("ep", None, "node"),
        P("ep", "node", None),
        P(("node", "ep"), None, None),
    )
    return jax.shard_map(
        shards, mesh=mesh, in_specs=placed, out_specs=P(("node", "ep"), None, None), check_vma=False
    )
```

profile of v0, /device:TPU:1, one launch (start us, length us, event | category | flops | bytes accessed | tf_op | source)
XLA Modules:
  0.0 204.9 jit_solution(8242603528993567378)
XLA Ops:
  0.0 1.0 copy.71
  1.0 0.7 broadcast_multiply_fusion
  1.9 1.5 reduce-window.6
  3.3 0.3 slice_reduce_fusion
  3.8 0.7 reshape.397
  4.5 0.9 fusion.55
  5.7 4.1 %scatter_custom_fusion = s32[768]{0:T(1024)S(1)} fusion(s32[514]{0:T(1024)S(1)} %fusion.59, s32[514]{0:T(1024)S(1)} %add_select_fusion, s32[]{:T(128)} %constant.77.clone.1), kind=kCustom, calls=%fused_computation.81 | custom fusion | bytes 3076 | tf_op jit(solution)/shard_map/scatter | solution.py:75
  9.8 1.3 convert_reduce_fusion
  11.1 1.4 fusion.46
  12.6 4.2 %convolution_convert_fusion.1 = bf16[257,1280]{1,0:T(8,128)(2,1)} fusion(bf16[1280,1280]{1,0:T(8,128)(2,1)} %param.10, bf16[1,257,1280]{2,1,0:T(8,128)(2,1)} %param.9, f32[257]{0:T(512)S(1)} %add_rsqrt_fusion.1, f32[257]{0:T(512)S(1)} %broadcast_multiply_fusion.2), kind=kOutput, calls=%fused_computation.34 | convolution fusion | flops 843782400 | bytes 4594696 | tf_op jit(solution)/shard_map/ctd,de->cte/dot_general | solution.py:38
  16.7 2.2 %copy.82 = bf16[257,1280]{0,1:T(8,128)(2,1)} copy(bf16[257,1280]{1,0:T(8,128)(2,1)} %convolution_convert_fusion.1) | data formatting | bytes 1315840 | tf_op jit(solution)/shard_map/reshape.21
  19.0 4.1 %convolution_convert_fusion = bf16[257,1280]{1,0:T(8,128)(2,1)} fusion(bf16[1280,1280]{1,0:T(8,128)(2,1)} %param.11, bf16[1,257,1280]{2,1,0:T(8,128)(2,1)} %param.9, f32[257]{0:T(512)S(1)} %add_rsqrt_fusion.1, f32[257]{0:T(512)S(1)} %broadcast_multiply_fusion.2), kind=kOutput, calls=%fused_computation.33 | convolution fusion | flops 843782400 | bytes 4594696 | tf_op jit(solution)/shard_map/ctd,de->cte/dot_general | solution.py:41
  23.1 2.2 %copy.83 = bf16[257,1280]{0,1:T(8,128)(2,1)} copy(bf16[257,1280]{1,0:T(8,128)(2,1)} %convolution_convert_fusion) | data formatting | bytes 1315840 | tf_op jit(solution)/shard_map/reshape.22
  25.4 4.1 %convolution_convert_fusion.2 = bf16[257,1280]{1,0:T(8,128)(2,1)} fusion(bf16[1280,1280]{1,0:T(8,128)(2,1)} %param.12, bf16[1,257,1280]{2,1,0:T(8,128)(2,1)} %param.9, f32[257]{0:T(512)S(1)} %add_rsqrt_fusion.1, f32[257]{0:T(512)S(1)} %broadcast_multiply_fusion.2), kind=kOutput, calls=%fused_computation.35 | convolution fusion | flops 843782400 | bytes 4594696 | tf_op jit(solution)/shard_map/ctd,de->cte/dot_general | solution.py:44
  29.5 2.2 %copy.81 = bf16[257,1280]{0,1:T(8,128)(2,1)} copy(bf16[257,1280]{1,0:T(8,128)(2,1)} %convolution_convert_fusion.2) | data formatting | bytes 1315840 | tf_op jit(solution)/shard_map/reshape.28
  31.7 6.5 %fusion.70 = (f32[16,257]{1,0:T(8,128)S(1)}, f32[16,257,257]{1,2,0:T(8,128)}) fusion(bf16[257,16,80]{0,2,1:T(8,128)(2,1)} %bitcast.114, bf16[257,16,80]{0,2,1:T(8,128)(2,1)} %bitcast.115), kind=kOutput, calls=%fused_computation.93 | convolution fusion | flops 172256048 | bytes 5559424 | tf_op jit(solution)/shard_map/sub | solution.py:53
  38.2 4.2 %fusion.45 = bf16[16,80,257]{2,1,0:T(8,128)(2,1)S(1)} fusion(bf16[257,16,80]{0,2,1:T(8,128)(2,1)} %bitcast.116, f32[16,257,257]{1,2,0:T(8,128)} %get-tuple-element.8, f32[16,257]{1,0:T(8,128)S(1)} %get-tuple-element.7), kind=kOutput, calls=%fused_computation.42 | convolution fusion | flops 171527968 | bytes 5559424 | tf_op jit(solution)/shard_map/chqk,ckhd->cqhd/dot_general | solution.py:54
  42.4 1.2 fusion.71
  43.6 0.3 multiply_reduce_fusion.2
  43.9 0.7 copy-done.2
  44.7 0.2 fusion.49
  45.1 2.9 %gather_fusion = bf16[768,1280]{1,0:T(8,128)(2,1)S(1)} fusion(bf16[257,1280]{1,0:T(8,128)(2,1)S(1)} %fusion.49, s32[1024]{0:T(1024)S(1)} %pad_clamp_fusion.1), kind=kCustom, calls=%fused_computation | custom fusion | bytes 3935232 | tf_op jit(solution)/shard_map/jit(_take)/gather | solution.py:77
  48.0 0.3 select_select_fusion
  48.4 51.9 %all_to_all.10 = bf16[32,1,24,1280]{3,2,1,0:T(8,128)(2,1)S(1)} all-to-all(bf16[32,1,24,1280]{3,2,1,0:T(8,128)(2,1)S(1)} %select_select_fusion), channel_id=1, replica_groups=mesh['node'=1,'ep'=32] {'node','ep'}, dimensions={0} | all-to-all | bytes 3932160 | tf_op jit(solution)/shard_map/all_to_all | solution.py:82
  100.3 32.4 %fusion.28 = bf16[32,1,24,1280]{3,2,1,0:T(8,128)(2,1)} fusion(bf16[1,5120,1280]{2,1,0:T(8,128)(2,1)} %param.16, bf16[1,1280,5120]{2,1,0:T(8,128)(2,1)} %param.15, bf16[32,1,24,1280]{3,2,1,0:T(8,128)(2,1)S(1)} %all_to_all.10), kind=kOutput, calls=%fused_computation.28 | convolution fusion | flops 20169031680 | bytes 30146560 | tf_op jit(solution)/shard_map/lesf,efd->lesd/dot_general | solution.py:85
  132.7 4.5 %all-to-all-start.1 = ((bf16[32,1,24,1280]{3,2,1,0:T(8,128)(2,1)}), bf16[32,1,24,1280]{3,2,1,0:T(8,128)(2,1)S(1)}, u32[]{:S(2)}, u32[]{:S(2)}) async-start(bf16[32,1,24,1280]{3,2,1,0:T(8,128)(2,1)} %fusion.28), calls=%async_computation.1 | async-start | bytes 3932160 | tf_op jit(solution)/shard_map/all_to_all | solution.py:88
  137.4 0.3 fusion.73
  138.3 44.5 %all-to-all-done.1 = bf16[32,1,24,1280]{3,2,1,0:T(8,128)(2,1)S(1)} async-done(((bf16[32,1,24,1280]{3,2,1,0:T(8,128)(2,1)}), bf16[32,1,24,1280]{3,2,1,0:T(8,128)(2,1)S(1)}, u32[]{:S(2)}, u32[]{:S(2)}) %all-to-all-start.1) | async-done | bytes 1966112 | tf_op jit(solution)/shard_map/all_to_all | solution.py:88
  182.8 3.4 %gather_fusion.1 = bf16[514,1280]{1,0:T(8,128)(2,1)} fusion(bf16[768,1280]{1,0:T(8,128)(2,1)S(1)} %bitcast.112, s32[1024]{0:T(1024)S(1)} %pad_clamp_fusion), kind=kCustom, calls=%fused_computation.1 | custom fusion | bytes 2633736 | tf_op jit(solution)/shard_map/jit(_take)/gather | solution.py:94
  186.2 4.0 %gather.15 = bf16[1,257,2,1280]{3,2,1,0:T(2,128)(2,1)} reshape(bf16[514,1280]{1,0:T(8,128)(2,1)} %gather_fusion.1) | data formatting | bytes 2631680 | tf_op jit(solution)/shard_map/jit(_take)/gather | solution.py:94
  190.2 13.7 %multiply_reduce_fusion.1 = f32[257,1280]{1,0:T(8,128)S(1)} fusion(bf16[1,257,2,1280]{3,2,1,0:T(2,128)(2,1)} %gather.15, pred[257,2]{1,0:T(8,128)(4,1)S(1)} %copy.76, f32[257,2]{1,0:T(8,128)S(1)} %copy.70), kind=kLoop, calls=%fused_computation.31 | loop fusion | flops 2302720 | bytes 2634250 | tf_op jit(solution)/shard_map/reduce_sum | solution.py:95
  203.9 1.0 fusion.48
  (43 shorter events, 1.6 us)
Async XLA Ops:
  0.0 42.4 %copy-start = (bf16[1280,1280]{1,0:T(8,128)(2,1)S(1)}, bf16[1280,1280]{1,0:T(8,128)(2,1)}, u32[]{:S(2)}) copy-start(bf16[1280,1280]{1,0:T(8,128)(2,1)} %param.13) | copy-start | bytes 9830404
  38.2 4.2 %copy-start.4 = (bf16[1,257,1280]{2,1,0:T(8,128)(2,1)S(1)}, bf16[1,257,1280]{2,1,0:T(8,128)(2,1)}, u32[]{:S(2)}) copy-start(bf16[1,257,1280]{2,1,0:T(8,128)(2,1)} %param.9) | copy-start | bytes 1973764
  43.6 1.1 copy-start.2
  132.7 4.7 %copy-start.5 = (bf16[1280,32]{0,1:T(8,128)(2,1)S(1)}, bf16[1280,32]{0,1:T(8,128)(2,1)}, u32[]{:S(2)}) copy-start(bf16[1280,32]{0,1:T(8,128)(2,1)} %param.14) | copy-start | bytes 245764
  132.7 5.0 %copy-start.6 = (s32[1,257,2]{1,2,0:T(2,128)S(1)}, s32[1,257,2]{1,2,0:T(2,128)}, u32[]{:S(2)}) copy-start(s32[1,257,2]{1,2,0:T(2,128)} %param.17) | copy-start | bytes 6172
  132.7 50.0 %all-to-all-start.1 = ((bf16[32,1,24,1280]{3,2,1,0:T(8,128)(2,1)}), bf16[32,1,24,1280]{3,2,1,0:T(8,128)(2,1)S(1)}, u32[]{:S(2)}, u32[]{:S(2)}) async-start(bf16[32,1,24,1280]{3,2,1,0:T(8,128)(2,1)} %fusion.28), calls=%async_computation.1 | async-start | bytes 3932160 | tf_op jit(solution)/shard_map/all_to_all | solution.py:88
  190.2 13.7 %copy-start.3 = (f32[1,257,1280]{2,1,0:T(8,128)S(1)}, f32[1,257,1280]{2,1,0:T(8,128)}, u32[]{:S(2)}) copy-start(f32[1,257,1280]{2,1,0:T(8,128)} %copy-done.2) | copy-start | bytes 3947524
  190.2 14.7 %copy-start.1 = (bf16[1280,1280]{1,0:T(8,128)(2,1)S(1)}, bf16[1280,1280]{1,0:T(8,128)(2,1)}, u32[]{:S(2)}) copy-start(bf16[1280,1280]{1,0:T(8,128)(2,1)} %param.13) | copy-start | bytes 9830404
where the time goes:
time: 206 us; the launch traced here: 205 us
  matrix products  57.1 us (28%)
  blocking collectives  51.9 us (25%)
  waiting for transfers between devices  44.5 us (22%)
  local copies, waits for them, and re-layouts  25.1 us (12%)
  other arithmetic  21.5 us (10%)
  starting transfers between devices  4.51 us (2%)
    all_to_all x1, blocking collectives, shards(): lax.all_to_all(copies, ('node', 'ep'), split_axis=0, concat_axis=0, tiled...  51.9 us
    all_to_all x1, waiting for transfers between devices, shards(): lax.all_to_all(partial_sum, ('node', 'ep'), split_axis=0, concat_axis=0,...  44.5 us
    dot_general x1, matrix products, shards(): jnp.einsum('lesf,efd->lesd', hidden, w_out, preferred_element_type=jnp.fl...  32.4 us
    reduce_sum x1, other arithmetic, shards(): jnp.sum(gate_values[..., None] * picked.astype(jnp.float32), axis=2)  13.7 us
    another operation x8, local copies, waits for them, and re-layouts  7.5 us
    gather x2, local copies, waits for them, and re-layouts, shards(): jnp.take(result_rows, position, axis=0)  7.42 us
    sub x1, matrix products, shards(): weights = jax.nn.softmax(scores, axis=-1).astype(jnp.bfloat16)  6.49 us
    all_to_all x1, starting transfers between devices, shards(): lax.all_to_all(partial_sum, ('node', 'ep'), split_axis=0, concat_axis=0,...  4.51 us
  transfers between devices with their start and end apart: 1, of which 1 were waited for; matrix products, arithmetic and copies ran while one was open for 0% of the time, Pallas kernels for 0%

commit v1 on v0

v1 whole, which is shorter than its diff:
```python
import functools
import math

import jax
import jax.numpy as jnp
from jax import lax
from jax.experimental import pallas as pl
from jax.experimental.pallas import tpu as pltpu
from jax.sharding import PartitionSpec as P

HEAD = 80
CAP = 24
LANES = 128
TILE = 256
PLANES = 4
CHUNK = 8
VMEM_BYTES = 60 * 1024 * 1024
MESH = pl.DeviceIdType.MESH


def up_to(value, step):
    return (value + step - 1) // step * step


def layer_norm(values):
    center = values - jnp.mean(values, axis=-1, keepdims=True)
    spread = jnp.mean(center * center, axis=-1, keepdims=True)
    return center * lax.rsqrt(spread + 1e-06)


def choose(rows, experts, routes, table, which):
    columns = lax.broadcasted_iota(jnp.int32, (rows, experts), 1)
    return jnp.sum(jnp.where(routes[:, which : which + 1] == columns, table, 0.0), axis=1, keepdims=True)


def route(tokens, rows, wide, router_ref, routes_ref, middle, out_ref, gate_ref, place_ref, normed, wanted):
    width = middle.shape[1]
    experts = router_ref.shape[1]
    slots = experts * CAP
    normed[rows:, :] = jnp.zeros((wide - rows, width), jnp.bfloat16)
    normed[:rows, :] = layer_norm(middle[...]).astype(jnp.bfloat16)
    wanted[...] = jnp.full((wide, 2), -1, jnp.int32)
    wanted[:tokens, :] = routes_ref[0]
    routes_wide = wanted[...]
    routes = routes_wide[:rows, :]
    logits = jnp.dot(normed[:rows, :], router_ref[...], preferred_element_type=jnp.float32)
    columns = lax.broadcasted_iota(jnp.int32, (wide, experts), 1)
    named = jnp.where(routes_wide[:, 0:1] == columns, 1.0, 0.0) + jnp.where(
        routes_wide[:, 1:2] == columns, 1.0, 0.0
    )
    earlier = jnp.where(
        lax.broadcasted_iota(jnp.int32, (rows, wide), 1) < lax.broadcasted_iota(jnp.int32, (rows, wide), 0),
        1.0,
        0.0,
    ).astype(jnp.bfloat16)
    rank = jnp.dot(earlier, named.astype(jnp.bfloat16), preferred_element_type=jnp.float32)
    slot_of = lax.broadcasted_iota(jnp.int32, (rows, slots), 1)
    sends = jnp.zeros((rows, slots), jnp.float32)
    for which in range(2):
        chosen = choose(rows, experts, routes, logits, which)
        gate_ref[:, which : which + 1] = jax.nn.sigmoid(chosen)
        turn = choose(rows, experts, routes, rank, which).astype(jnp.int32)
        place = routes[:, which : which + 1] * CAP + turn
        place_ref[:, which : which + 1] = place
        sends = sends + jnp.where(place == slot_of, 1.0, 0.0)
    sends = jnp.concatenate([sends, jnp.zeros((wide - rows, slots), jnp.float32)], axis=0)
    picks = jnp.transpose(sends).astype(jnp.bfloat16)

    @pl.loop(0, width // TILE)
    def _(tile):
        part = pl.ds(pl.multiple_of(tile * TILE, TILE), TILE)
        block = jnp.dot(picks, normed[:, part], preferred_element_type=jnp.float32)
        out_ref[:, :, part] = block.reshape(experts, CAP, TILE).astype(jnp.bfloat16)


def attend_kernel(
    tokens, images_ref, q_hbm, k_hbm, v_hbm, o_hbm, router_ref, routes_ref,
    out_ref, middle_ref, gate_ref, place_ref,
    weights, sems, inputs, normed, queries, keys, values, mixed, second, wanted,
):
    rows, width = inputs.shape
    wide = keys.shape[0]
    loads = [
        pltpu.make_async_copy(source, weights.at[at], sems.at[at])
        for at, source in enumerate((q_hbm, k_hbm, v_hbm, o_hbm))
    ]
    for load in loads:
        load.start()
    inputs[...] = jnp.zeros((rows, width), jnp.float32)
    inputs[:tokens, :] = images_ref[0].astype(jnp.float32)
    normed[...] = layer_norm(inputs[...]).astype(jnp.bfloat16)
    mixed[...] = jnp.zeros((rows, width), jnp.float32)
    keys[rows:, :] = jnp.zeros((wide - rows, width), jnp.bfloat16)
    values[rows:, :] = jnp.zeros((wide - rows, width), jnp.bfloat16)
    for at, target in enumerate((queries, keys, values)):
        loads[at].wait()

        @pl.loop(0, width // TILE)
        def _(tile):
            part = pl.ds(pl.multiple_of(tile * TILE, TILE), TILE)
            target[:rows, part] = jnp.dot(
                normed[...], weights[at, :, part], preferred_element_type=jnp.float32
            ).astype(jnp.bfloat16)

    period = math.lcm(HEAD, LANES)
    valid = lax.broadcasted_iota(jnp.int32, (rows, wide), 1) < tokens

    @pl.loop(0, width // period)
    def _(turn):
        for head in range(period // HEAD):
            low = head * HEAD // LANES * LANES
            span = up_to(head * HEAD + HEAD, LANES) - low
            part = pl.ds(pl.multiple_of(turn * period + low, LANES), span)
            lane = lax.broadcasted_iota(jnp.int32, (rows, span), 1) + low
            inside = (lane >= head * HEAD) & (lane < head * HEAD + HEAD)
            query = jnp.where(inside, queries[:, part].astype(jnp.float32), 0.0).astype(jnp.bfloat16)
            scores = lax.dot_general(
                query, keys[:, part], (((1,), (1,)), ((), ())), preferred_element_type=jnp.float32
            ) * (1.0 / math.sqrt(HEAD))
            scores = jnp.where(valid, scores, -1e30)
            raised = jnp.exp(scores - jnp.max(scores, axis=1, keepdims=True))
            raised = jnp.where(valid, raised, 0.0)
            probs = (raised * (1.0 / jnp.sum(raised, axis=1, keepdims=True))).astype(jnp.bfloat16)
            result = jnp.dot(probs, values[:, part], preferred_element_type=jnp.float32)
            mixed[:, part] += jnp.where(inside, result, 0.0)

    normed[...] = mixed[...].astype(jnp.bfloat16)
    loads[3].wait()

    @pl.loop(0, width // TILE)
    def _(tile):
        part = pl.ds(pl.multiple_of(tile * TILE, TILE), TILE)
        middle_ref[:, part] = inputs[:, part] + jnp.dot(
            normed[...], weights[3, :, part], preferred_element_type=jnp.float32
        )

    route(tokens, rows, wide, router_ref, routes_ref, middle_ref, out_ref, gate_ref, place_ref, second, wanted)


def route_kernel(tokens, middle_ref, router_ref, routes_ref, out_ref, gate_ref, place_ref, second, wanted):
    rows, wide = middle_ref.shape[0], second.shape[0]
    route(tokens, rows, wide, router_ref, routes_ref, middle_ref, out_ref, gate_ref, place_ref, second, wanted)


def expert_kernel(
    node_count, columns, out_ref, in_hbm, down_hbm, back_ref,
    first, second, arrived, results, total, weight_sems, go_send, go_recv, back_send, back_recv,
):
    number = node_count * columns
    plane = number // PLANES
    chunks = number // CHUNK
    own_slot = 4
    me = lax.axis_index("node") * columns + lax.axis_index("ep")
    loads = [
        pltpu.make_async_copy(in_hbm.at[0], first, weight_sems.at[0]),
        pltpu.make_async_copy(down_hbm.at[0], second, weight_sems.at[1]),
    ]
    for load in loads:
        load.start()

    def offset(slot):
        within = slot % CHUNK
        return (within // 2 + 2) % PLANES * plane + slot // CHUNK * 2 + within % 2

    def name(device):
        return (device // columns, device % columns)

    def go(slot):
        target = (me + offset(slot)) % number
        return pltpu.make_async_remote_copy(
            src_ref=out_ref.at[target % columns],
            dst_ref=arrived.at[slot],
            send_sem=go_send.at[slot],
            recv_sem=go_recv.at[slot],
            device_id=name(target),
            device_id_type=MESH,
        )

    def back(slot):
        source = (me - offset(slot) + number) % number
        return pltpu.make_async_remote_copy(
            src_ref=results.at[slot],
            dst_ref=back_ref.at[me],
            send_sem=back_send.at[slot],
            recv_sem=back_recv.at[slot],
            device_id=name(source),
            device_id_type=MESH,
        )

    def landed(slot):
        source = (me + offset(slot)) % number
        return pltpu.make_async_remote_copy(
            src_ref=results.at[slot],
            dst_ref=back_ref.at[source],
            send_sem=back_send.at[slot],
            recv_sem=back_recv.at[slot],
            device_id=name(source),
            device_id_type=MESH,
        )

    barrier = pltpu.get_barrier_semaphore()

    @pl.loop(1, number)
    def _(step):
        pl.semaphore_signal(barrier, inc=1, device_id=name((me + step) % number), device_id_type=MESH)

    pl.semaphore_wait(barrier, number - 1)

    @pl.loop(0, number)
    def _(slot):
        @pl.when(slot != own_slot)
        def _():
            go(slot).start()

    arrived[own_slot] = out_ref[me % columns]
    for load in loads:
        load.wait()
    width, hidden_units = first.shape
    section = width if hidden_units % width == 0 else hidden_units

    @pl.loop(0, chunks)
    def _(chunk):
        for within in range(CHUNK):
            slot = chunk * CHUNK + within

            @pl.when(slot != own_slot)
            def _():
                go(slot).wait_recv()

        held = pl.ds(chunk * CHUNK, CHUNK)
        buffer = arrived[held].astype(jnp.float32).reshape(CHUNK * CAP, width).astype(jnp.bfloat16)
        total[...] = jnp.zeros_like(total)

        @pl.loop(0, hidden_units // section)
        def _(at):
            part = pl.ds(pl.multiple_of(at * section, section), section)
            before = jnp.dot(buffer, first[:, part], preferred_element_type=jnp.float32)
            hidden = jax.nn.gelu(before, approximate=True).astype(jnp.bfloat16)
            total[...] += jnp.dot(hidden, second[part, :], preferred_element_type=jnp.float32)

        results[held] = total[...].reshape(CHUNK, CAP, width).astype(jnp.bfloat16)
        for within in range(CHUNK):
            slot = chunk * CHUNK + within

            @pl.when(slot != own_slot)
            def _():
                back(slot).start()

    back_ref[me] = results[own_slot]

    @pl.loop(0, number)
    def _(slot):
        @pl.when(slot != own_slot)
        def _():
            go(slot).wait_send()
            back(slot).wait_send()
            landed(slot).wait_recv()


def combine_kernel(tokens, middle_ref, gate_ref, place_ref, back_ref, out_ref):
    rows, width = middle_ref.shape
    experts = back_ref.shape[0]
    slots = experts * CAP
    slot_of = lax.broadcasted_iota(jnp.int32, (rows, slots), 1)
    picks = [
        jnp.where(place_ref[:, which : which + 1] == slot_of, 1.0, 0.0).astype(jnp.bfloat16)
        for which in range(2)
    ]

    @pl.loop(0, width // TILE)
    def _(tile):
        part = pl.ds(pl.multiple_of(tile * TILE, TILE), TILE)
        block = back_ref[:, :, part].astype(jnp.float32).reshape(slots, TILE).astype(jnp.bfloat16)
        value = middle_ref[:, part]
        mix = jnp.zeros_like(value)
        for which in range(2):
            mix = mix + gate_ref[:, which : which + 1] * jnp.dot(
                picks[which], block, preferred_element_type=jnp.float32
            )
        out_ref[0, :, part] = (value + mix)[:tokens, :].astype(jnp.bfloat16)


def attention_over_nodes(images, w_query, w_key, w_value, w_output):
    local_heads = w_query.shape[1] // HEAD
    inputs = images.astype(jnp.float32)
    normed = layer_norm(inputs).astype(jnp.bfloat16)
    gathered = lax.all_gather(normed, "node", axis=0, tiled=True)
    number, tokens, _ = gathered.shape

    def project(weight):
        result = jnp.einsum("ctd,de->cte", gathered, weight, preferred_element_type=jnp.float32)
        return result.astype(jnp.bfloat16).reshape(number, tokens, local_heads, HEAD)

    scores = jnp.einsum(
        "cqhd,ckhd->chqk", project(w_query), project(w_key), preferred_element_type=jnp.float32
    ) / math.sqrt(HEAD)
    probs = jax.nn.softmax(scores, axis=-1).astype(jnp.bfloat16)
    mixture = jnp.einsum(
        "chqk,ckhd->cqhd", probs, project(w_value), preferred_element_type=jnp.float32
    ).astype(jnp.bfloat16)
    mixture = mixture.reshape(number, tokens, local_heads * HEAD)
    mixture = lax.all_to_all(mixture, "node", split_axis=0, concat_axis=2, tiled=True)
    return inputs + jnp.einsum("itd,de->ite", mixture, w_output, preferred_element_type=jnp.float32)


def shards(images, w_query, w_key, w_value, w_output, router, w_in, w_out, routes):
    _, tokens, width = images.shape
    node_count = lax.axis_size("node")
    columns = lax.axis_size("ep")
    number = node_count * columns
    experts = router.shape[1]
    hidden_units = w_in.shape[2]
    rows, wide = up_to(tokens, 16), up_to(tokens, LANES)
    here = pl.BlockSpec(memory_space=pltpu.VMEM)
    anywhere = pl.BlockSpec(memory_space=pl.ANY)
    params = pltpu.CompilerParams(vmem_limit_bytes=VMEM_BYTES)
    blocks = jax.ShapeDtypeStruct((experts, CAP, width), jnp.bfloat16)
    middle_shape = jax.ShapeDtypeStruct((rows, width), jnp.float32)
    small = [jax.ShapeDtypeStruct((rows, 2), jnp.float32), jax.ShapeDtypeStruct((rows, 2), jnp.int32)]
    route_scratch = [pltpu.VMEM((wide, width), jnp.bfloat16), pltpu.VMEM((wide, 2), jnp.int32)]
    if node_count == 1:
        outgoing, middle, gates, places = pl.pallas_call(
            functools.partial(attend_kernel, tokens),
            out_shape=[blocks, middle_shape] + small,
            in_specs=[here] + [anywhere] * 4 + [here] * 2,
            out_specs=[here] * 4,
            scratch_shapes=[
                pltpu.VMEM((4, width, width), jnp.bfloat16),
                pltpu.SemaphoreType.DMA((4,)),
                pltpu.VMEM((rows, width), jnp.float32),
                pltpu.VMEM((rows, width), jnp.bfloat16),
                pltpu.VMEM((rows, width), jnp.bfloat16),
                pltpu.VMEM((wide, width), jnp.bfloat16),
                pltpu.VMEM((wide, width), jnp.bfloat16),
                pltpu.VMEM((rows, width), jnp.float32),
            ] + route_scratch,
            compiler_params=params,
            name="attend",
        )(images, w_query, w_key, w_value, w_output, router, routes)
    else:
        middle = attention_over_nodes(images, w_query, w_key, w_value, w_output)[0]
        middle = jnp.pad(middle, ((0, rows - tokens), (0, 0)))
        outgoing, gates, places = pl.pallas_call(
            functools.partial(route_kernel, tokens),
            out_shape=[blocks] + small,
            in_specs=[here] * 3,
            out_specs=[here] * 3,
            scratch_shapes=route_scratch,
            compiler_params=params,
            name="route",
        )(middle, router, routes)
    returned = pl.pallas_call(
        functools.partial(expert_kernel, node_count, columns),
        out_shape=jax.ShapeDtypeStruct((number, CAP, width), jnp.bfloat16),
        in_specs=[here, anywhere, anywhere],
        out_specs=here,
        scratch_shapes=[
            pltpu.VMEM((width, hidden_units), jnp.bfloat16),
            pltpu.VMEM((hidden_units, width), jnp.bfloat16),
            pltpu.VMEM((number, CAP, width), jnp.bfloat16),
            pltpu.VMEM((number, CAP, width), jnp.bfloat16),
            pltpu.VMEM((CHUNK * CAP, width), jnp.float32),
            pltpu.SemaphoreType.DMA((2,)),
            pltpu.SemaphoreType.DMA((number,)),
            pltpu.SemaphoreType.DMA((number,)),
            pltpu.SemaphoreType.DMA((number,)),
            pltpu.SemaphoreType.DMA((number,)),
        ],
        compiler_params=pltpu.CompilerParams(
            collective_id=0, has_side_effects=True, vmem_limit_bytes=VMEM_BYTES
        ),
        name="experts",
    )(outgoing, w_in, w_out)
    if node_count > 1:
        summed = jnp.sum(returned.astype(jnp.float32).reshape(node_count, experts, CAP, width), axis=0)
        returned = summed.astype(jnp.bfloat16)
    return pl.pallas_call(
        functools.partial(combine_kernel, tokens),
        out_shape=jax.ShapeDtypeStruct(images.shape, jnp.bfloat16),
        in_specs=[here] * 4,
        out_specs=here,
        compiler_params=params,
        name="combine",
    )(middle, gates, places, returned)


def solution(mesh):
    placed = (
        P(("node", "ep"), None, None),
        P(None, "node"),
        P(None, "node"),
        P(None, "node"),
        P(),
        P(),
        P("ep", None, "node"),
        P("ep", "node", None),
        P(("node", "ep"), None, None),
    )
    return jax.shard_map(
        shards, mesh=mesh, in_specs=placed, out_specs=P(("node", "ep"), None, None), check_vma=False
    )
```

time: 206 us -> 125 us (0.61)
  Pallas kernels: 0 us -> 122 us
  matrix products: 57.1 us -> 0 us
  blocking collectives: 51.9 us -> 0 us
  waiting for transfers between devices: 44.5 us -> 0 us
  local copies, waits for them, and re-layouts: 25.1 us -> 3.26 us
  other arithmetic: 21.5 us -> 0 us
  starting transfers between devices: 4.51 us -> 0 us
    pallas_call x0 -> x3, Pallas kernels: none -> 122 us  [the longest x1 96.9 us: shards(): pl.pallas_call(functools.partial(expert_kernel, node_count, columns), out...]
    all_to_all x1 -> x0, blocking collectives: 51.9 us -> none  [shards(): lax.all_to_all(copies, ('node', 'ep'), split_axis=0, concat_axis=0, tiled...]
    dot_general x7 -> x0, matrix products: 50.6 us -> none  [the longest x1 32.4 us: shards(): jnp.einsum('lesf,efd->lesd', hidden, w_out, preferred_element_type=jnp.fl...]
    all_to_all x1 -> x0, waiting for transfers between devices: 44.5 us -> none  [shards(): lax.all_to_all(partial_sum, ('node', 'ep'), split_axis=0, concat_axis=0,...]
    reduce_sum x6 -> x0, other arithmetic: 16.8 us -> none  [the longest x1 13.7 us: shards(): jnp.sum(gate_values[..., None] * picked.astype(jnp.float32), axis=2)]
    gather x3 -> x0, local copies, waits for them, and re-layouts: 10.3 us -> none  [the longest x2 7.42 us: shards(): jnp.take(result_rows, position, axis=0)]
    another operation x8 -> x0, local copies, waits for them, and re-layouts: 7.5 us -> none
    sub x1 -> x0, matrix products: 6.49 us -> none  [shards(): weights = jax.nn.softmax(scores, axis=-1).astype(jnp.bfloat16)]
  transfers between devices with their start and end apart: 1 -> 0, of which waited for: 1 -> 0; matrix products, arithmetic and copies ran while one was open for 0% -> 0% of each run, Pallas kernels for 0% -> 0%
where the time goes in v1:
time: 125 us
  Pallas kernels  122 us (98%)
  local copies, waits for them, and re-layouts  3.26 us (3%)
    pallas_call x1, Pallas kernels, shards(): pl.pallas_call(functools.partial(expert_kernel, node_count, columns), out...  96.9 us
    pallas_call x1, Pallas kernels, shards(): pl.pallas_call(functools.partial(attend_kernel, tokens), out_shape=[block...  19.6 us
    pallas_call x1, Pallas kernels, shards(): pl.pallas_call(functools.partial(combine_kernel, tokens), out_shape=jax.S...  5.15 us
    unnamed x2, local copies, waits for them, and re-layouts  3.26 us

profile of v1, /device:TPU:1, one launch (start us, length us, event | category | flops | bytes accessed | tf_op | source)
XLA Modules:
  0.0 124.9 jit_solution(14193942368450217762)
XLA Ops:
  0.0 1.5 %copy.11.routes_ref = s32[1,257,2]{2,1,0:T(8,128)} copy(s32[1,257,2]{1,2,0:T(2,128)} %param.17) | data formatting | bytes 4112 | tf_op args[8]
  1.5 1.8 %copy.10.router_ref = bf16[1280,32]{1,0:T(8,128)(2,1)} copy(bf16[1280,32]{0,1:T(8,128)(2,1)} %param.14) | data formatting | bytes 163840 | tf_op args[5]
  3.3 19.6 %attend.1 = (bf16[32,24,1280]{2,1,0:T(8,128)(2,1)}, f32[272,1280]{1,0:T(8,128)}, f32[272,2]{1,0:T(8,128)}, s32[272,2]{1,0:T(8,128)}) custom-call(bf16[1,257,1280]{2,1,0:T(8,128)(2,1)} %images_ref.1, bf16[1280,1280]{1,0:T(8,128)(2,1)} %q_hbm.1, bf16[1280,1280]{1,0:T(8,128)(2,1)} %k_hbm.1, bf16[1280,1280]{1,0:T(8,128)(2,1)} %v_hbm.1, ...), custom_call_target="tpu_custom_call" | custom-call | tf_op jit(solution)/shard_map/attend/pallas_call | solution.py:322
  22.9 96.9 %experts.1.back_ref = bf16[32,24,1280]{2,1,0:T(8,128)(2,1)} custom-call(bf16[32,24,1280]{2,1,0:T(8,128)(2,1)} %get-tuple-element.12.out_ref, bf16[1,1280,5120]{2,1,0:T(8,128)(2,1)} %in_hbm.1, bf16[1,5120,1280]{2,1,0:T(8,128)(2,1)} %down_hbm.1), custom_call_target="tpu_custom_call" | custom-call | tf_op jit(solution)/shard_map/experts/pallas_call | solution.py:352
  119.8 5.1 %combine.1 = bf16[1,257,1280]{2,1,0:T(8,128)(2,1)} custom-call(f32[272,1280]{1,0:T(8,128)} %get-tuple-element.9.middle_ref, f32[272,2]{1,0:T(8,128)} %get-tuple-element.10.gate_ref, s32[272,2]{1,0:T(8,128)} %get-tuple-element.11.place_ref, bf16[32,24,1280]{2,1,0:T(8,128)(2,1)} %experts.1.back_ref), custom_call_target="tpu_custom_call" | custom-call | tf_op jit(solution)/shard_map/combine/pallas_call | solution.py:377

commit v2 on v1

--- a/solution.py
+++ b/solution.py
@@ -33,17 +33,19 @@
     return jnp.sum(jnp.where(routes[:, which : which + 1] == columns, table, 0.0), axis=1, keepdims=True)
 
 
-def route(tokens, rows, wide, router_ref, routes_ref, middle, out_ref, gate_ref, place_ref, normed, wanted):
+def route(tokens, rows, wide, router_ref, routes_ref, middle, out_ref, gate_ref, place_ref, normed, wanted, turned=None):
     width = middle.shape[1]
-    experts = router_ref.shape[1]
+    experts = router_ref.shape[0]
     slots = experts * CAP
     normed[rows:, :] = jnp.zeros((wide - rows, width), jnp.bfloat16)
     normed[:rows, :] = layer_norm(middle[...]).astype(jnp.bfloat16)
-    wanted[...] = jnp.full((wide, 2), -1, jnp.int32)
-    wanted[:tokens, :] = routes_ref[0]
-    routes_wide = wanted[...]
+    wanted[...] = jnp.full(wanted.shape, -1.0, jnp.float32)
+    wanted[0:2, :tokens] = routes_ref[...].astype(jnp.float32)
+    routes_wide = jnp.transpose(wanted[...]).astype(jnp.int32)
     routes = routes_wide[:rows, :]
-    logits = jnp.dot(normed[:rows, :], router_ref[...], preferred_element_type=jnp.float32)
+    logits = lax.dot_general(
+        normed[:rows, :], router_ref[...], (((1,), (1,)), ((), ())), preferred_element_type=jnp.float32
+    )
     columns = lax.broadcasted_iota(jnp.int32, (wide, experts), 1)
     named = jnp.where(routes_wide[:, 0:1] == columns, 1.0, 0.0) + jnp.where(
         routes_wide[:, 1:2] == columns, 1.0, 0.0
@@ -61,7 +63,10 @@
         gate_ref[:, which : which + 1] = jax.nn.sigmoid(chosen)
         turn = choose(rows, experts, routes, rank, which).astype(jnp.int32)
         place = routes[:, which : which + 1] * CAP + turn
-        place_ref[:, which : which + 1] = place
+        kept = place
+        if turned is not None:
+            kept = turned(routes[:, which : which + 1]) * CAP + turn
+        place_ref[:, which : which + 1] = kept
         sends = sends + jnp.where(place == slot_of, 1.0, 0.0)
     sends = jnp.concatenate([sends, jnp.zeros((wide - rows, slots), jnp.float32)], axis=0)
     picks = jnp.transpose(sends).astype(jnp.bfloat16)
@@ -73,19 +78,9 @@
         out_ref[:, :, part] = block.reshape(experts, CAP, TILE).astype(jnp.bfloat16)
 
 
-def attend_kernel(
-    tokens, images_ref, q_hbm, k_hbm, v_hbm, o_hbm, router_ref, routes_ref,
-    out_ref, middle_ref, gate_ref, place_ref,
-    weights, sems, inputs, normed, queries, keys, values, mixed, second, wanted,
-):
+def attend(tokens, images_ref, loads, weights, middle_ref, inputs, normed, queries, keys, values, mixed):
     rows, width = inputs.shape
     wide = keys.shape[0]
-    loads = [
-        pltpu.make_async_copy(source, weights.at[at], sems.at[at])
-        for at, source in enumerate((q_hbm, k_hbm, v_hbm, o_hbm))
-    ]
-    for load in loads:
-        load.start()
     inputs[...] = jnp.zeros((rows, width), jnp.float32)
     inputs[:tokens, :] = images_ref[0].astype(jnp.float32)
     normed[...] = layer_norm(inputs[...]).astype(jnp.bfloat16)
@@ -98,8 +93,9 @@
         @pl.loop(0, width // TILE)
         def _(tile):
             part = pl.ds(pl.multiple_of(tile * TILE, TILE), TILE)
+            taken = pl.ds(pl.multiple_of(at * width + tile * TILE, TILE), TILE)
             target[:rows, part] = jnp.dot(
-                normed[...], weights[at, :, part], preferred_element_type=jnp.float32
+                normed[...], weights[:, taken], preferred_element_type=jnp.float32
             ).astype(jnp.bfloat16)
 
     period = math.lcm(HEAD, LANES)
@@ -130,11 +126,10 @@
     @pl.loop(0, width // TILE)
     def _(tile):
         part = pl.ds(pl.multiple_of(tile * TILE, TILE), TILE)
+        taken = pl.ds(pl.multiple_of(3 * width + tile * TILE, TILE), TILE)
         middle_ref[:, part] = inputs[:, part] + jnp.dot(
-            normed[...], weights[3, :, part], preferred_element_type=jnp.float32
+            normed[...], weights[:, taken], preferred_element_type=jnp.float32
         )
-
-    route(tokens, rows, wide, router_ref, routes_ref, middle_ref, out_ref, gate_ref, place_ref, second, wanted)
 
 
 def route_kernel(tokens, middle_ref, router_ref, routes_ref, out_ref, gate_ref, place_ref, second, wanted):
@@ -142,21 +137,34 @@
     route(tokens, rows, wide, router_ref, routes_ref, middle_ref, out_ref, gate_ref, place_ref, second, wanted)
 
 
-def expert_kernel(
-    node_count, columns, out_ref, in_hbm, down_hbm, back_ref,
-    first, second, arrived, results, total, weight_sems, go_send, go_recv, back_send, back_recv,
+def place_of(node_count, columns):
+    return lax.axis_index("node") * columns + lax.axis_index("ep")
+
+
+def greet(node_count, columns):
+    number = node_count * columns
+    me = place_of(node_count, columns)
+    barrier = pltpu.get_barrier_semaphore()
+
+    @pl.loop(1, number)
+    def _(step):
+        peer = (me + step) % number
+        pl.semaphore_signal(
+            barrier, inc=1, device_id=(peer // columns, peer % columns), device_id_type=MESH
+        )
+
+    return lambda: pl.semaphore_wait(barrier, number - 1)
+
+
+def exchange(
+    node_count, columns, out_ref, loads, back_ref,
+    first, second, arrived, results, total, go_send, go_recv, back_send, back_recv, taken=None,
 ):
     number = node_count * columns
     plane = number // PLANES
     chunks = number // CHUNK
     own_slot = 4
-    me = lax.axis_index("node") * columns + lax.axis_index("ep")
-    loads = [
-        pltpu.make_async_copy(in_hbm.at[0], first, weight_sems.at[0]),
-        pltpu.make_async_copy(down_hbm.at[0], second, weight_sems.at[1]),
-    ]
-    for load in loads:
-        load.start()
+    me = place_of(node_count, columns)
 
     def offset(slot):
         within = slot % CHUNK
@@ -180,7 +188,7 @@
         source = (me - offset(slot) + number) % number
         return pltpu.make_async_remote_copy(
             src_ref=results.at[slot],
-            dst_ref=back_ref.at[me],
+            dst_ref=back_ref.at[slot],
             send_sem=back_send.at[slot],
             recv_sem=back_recv.at[slot],
             device_id=name(source),
@@ -191,20 +199,12 @@
         source = (me + offset(slot)) % number
         return pltpu.make_async_remote_copy(
             src_ref=results.at[slot],
-            dst_ref=back_ref.at[source],
+            dst_ref=back_ref.at[slot],
             send_sem=back_send.at[slot],
             recv_sem=back_recv.at[slot],
             device_id=name(source),
             device_id_type=MESH,
         )
-
-    barrier = pltpu.get_barrier_semaphore()
-
-    @pl.loop(1, number)
-    def _(step):
-        pl.semaphore_signal(barrier, inc=1, device_id=name((me + step) % number), device_id_type=MESH)
-
-    pl.semaphore_wait(barrier, number - 1)
 
     @pl.loop(0, number)
     def _(slot):
@@ -246,7 +246,19 @@
             def _():
                 back(slot).start()
 
-    back_ref[me] = results[own_slot]
+    back_ref[own_slot] = results[own_slot]
+
+    @pl.loop(0, chunks)
+    def _(chunk):
+        for within in range(CHUNK):
+            slot = chunk * CHUNK + within
+
+            @pl.when(slot != own_slot)
+            def _():
+                landed(slot).wait_recv()
+
+        if taken is not None:
+            taken(chunk)
 
     @pl.loop(0, number)
     def _(slot):
@@ -254,7 +266,82 @@
         def _():
             go(slot).wait_send()
             back(slot).wait_send()
-            landed(slot).wait_recv()
+
+
+def slot_for(expert, me, columns):
+    plane = columns // PLANES
+    away = (expert - me + columns) & (columns - 1)
+    ahead, step = away // plane, away & (plane - 1)
+    return step // 2 * CHUNK + ((ahead + PLANES - 2) & (PLANES - 1)) * 2 + (step & 1)
+
+
+def layer_kernel(
+    tokens, columns, images_ref, q_hbm, k_hbm, v_hbm, o_hbm, router_ref, routes_ref, in_hbm, down_hbm, result_ref,
+    first, second, outgoing, arrived, results, returned, total, middle, gates, places,
+    inputs, normed, queries, keys, values, mixed, normed_second, wanted,
+    load_sems, go_send, go_recv, back_send, back_recv,
+):
+    rows, width = inputs.shape
+    wide = keys.shape[0]
+    loads = [
+        pltpu.make_async_copy(source, first.at[:, pl.ds(at * width, width)], load_sems.at[at])
+        for at, source in enumerate((q_hbm, k_hbm, v_hbm, o_hbm))
+    ]
+    for load in loads:
+        load.start()
+    down = pltpu.make_async_copy(down_hbm.at[0], second, load_sems.at[4])
+    up = pltpu.make_async_copy(in_hbm.at[0], first, load_sems.at[5])
+    down.start()
+    met = greet(1, columns)
+    attend(tokens, images_ref, loads, first, middle, inputs, normed, queries, keys, values, mixed)
+    up.start()
+    me = place_of(1, columns)
+    route(
+        tokens, rows, wide, router_ref, routes_ref, middle, outgoing, gates, places, normed_second, wanted,
+        lambda expert: slot_for(expert, me, columns),
+    )
+    met()
+    span = CHUNK * CAP
+
+    def taken(chunk):
+        column = lax.broadcasted_iota(jnp.int32, (rows, span), 1) + chunk * span
+        picks = [
+            jnp.where(places[:, which : which + 1] == column, 1.0, 0.0).astype(jnp.bfloat16)
+            for which in range(2)
+        ]
+        blocks = returned[pl.ds(chunk * CHUNK, CHUNK)].astype(jnp.float32)
+        blocks = blocks.reshape(span, width).astype(jnp.bfloat16)
+        for tile in range(width // TILE):
+            part = pl.ds(tile * TILE, TILE)
+            mix = middle[:, part]
+            for which in range(2):
+                mix = mix + gates[:, which : which + 1] * jnp.dot(
+                    picks[which], blocks[:, tile * TILE : (tile + 1) * TILE], preferred_element_type=jnp.float32
+                )
+            middle[:, part] = mix
+
+    exchange(
+        1, columns, outgoing, [down, up], returned,
+        first, second, arrived, results, total, go_send, go_recv, back_send, back_recv, taken,
+    )
+    result_ref[0] = middle[:tokens, :].astype(jnp.bfloat16)
+
+
+def expert_kernel(
+    node_count, columns, out_ref, in_hbm, down_hbm, back_ref,
+    first, second, arrived, results, total, load_sems, go_send, go_recv, back_send, back_recv,
+):
+    loads = [
+        pltpu.make_async_copy(in_hbm.at[0], first, load_sems.at[0]),
+        pltpu.make_async_copy(down_hbm.at[0], second, load_sems.at[1]),
+    ]
+    for load in loads:
+        load.start()
+    greet(node_count, columns)()
+    exchange(
+        node_count, columns, out_ref, loads, back_ref,
+        first, second, arrived, results, total, go_send, go_recv, back_send, back_recv,
+    )
 
 
 def combine_kernel(tokens, middle_ref, gate_ref, place_ref, back_ref, out_ref):
@@ -317,63 +404,67 @@
     blocks = jax.ShapeDtypeStruct((experts, CAP, width), jnp.bfloat16)
     middle_shape = jax.ShapeDtypeStruct((rows, width), jnp.float32)
     small = [jax.ShapeDtypeStruct((rows, 2), jnp.float32), jax.ShapeDtypeStruct((rows, 2), jnp.int32)]
-    route_scratch = [pltpu.VMEM((wide, width), jnp.bfloat16), pltpu.VMEM((wide, 2), jnp.int32)]
-    if node_count == 1:
-        outgoing, middle, gates, places = pl.pallas_call(
-            functools.partial(attend_kernel, tokens),
-            out_shape=[blocks, middle_shape] + small,
-            in_specs=[here] + [anywhere] * 4 + [here] * 2,
-            out_specs=[here] * 4,
-            scratch_shapes=[
-                pltpu.VMEM((4, width, width), jnp.bfloat16),
-                pltpu.SemaphoreType.DMA((4,)),
+    route_scratch = [pltpu.VMEM((wide, width), jnp.bfloat16), pltpu.VMEM((8, wide), jnp.float32)]
+    exchange_blocks = pltpu.VMEM((number, CAP, width), jnp.bfloat16)
+    weight_scratch = [
+        pltpu.VMEM((width, hidden_units), jnp.bfloat16),
+        pltpu.VMEM((hidden_units, width), jnp.bfloat16),
+    ]
+    total_scratch = pltpu.VMEM((CHUNK * CAP, width), jnp.float32)
+    remote_sems = [pltpu.SemaphoreType.DMA((number,))] * 4
+    remote_params = pltpu.CompilerParams(
+        collective_id=0, has_side_effects=True, vmem_limit_bytes=VMEM_BYTES
+    )
+    router_rows, route_rows = router.T, routes[0].T
+    if node_count == 1 and hidden_units >= 4 * width:
+        return pl.pallas_call(
+            functools.partial(layer_kernel, tokens, columns),
+            out_shape=jax.ShapeDtypeStruct(images.shape, jnp.bfloat16),
+            in_specs=[here] + [anywhere] * 4 + [here] * 2 + [anywhere] * 2,
+            out_specs=here,
+            scratch_shapes=weight_scratch + [exchange_blocks] * 4 + [
+                total_scratch,
+                pltpu.VMEM((rows, width), jnp.float32),
+                pltpu.VMEM((rows, 2), jnp.float32),
+                pltpu.VMEM((rows, 2), jnp.int32),
                 pltpu.VMEM((rows, width), jnp.float32),
                 pltpu.VMEM((rows, width), jnp.bfloat16),
                 pltpu.VMEM((rows, width), jnp.bfloat16),
                 pltpu.VMEM((wide, width), jnp.bfloat16),
                 pltpu.VMEM((wide, width), jnp.bfloat16),
                 pltpu.VMEM((rows, width), jnp.float32),
-            ] + route_scratch,
-            compiler_params=params,
-            name="attend",
-        )(images, w_query, w_key, w_value, w_output, router, routes)
-    else:
-        middle = attention_over_nodes(images, w_query, w_key, w_value, w_output)[0]
-        middle = jnp.pad(middle, ((0, rows - tokens), (0, 0)))
-        outgoing, gates, places = pl.pallas_call(
-            functools.partial(route_kernel, tokens),
-            out_shape=[blocks] + small,
-            in_specs=[here] * 3,
-            out_specs=[here] * 3,
-            scratch_shapes=route_scratch,
-            compiler_params=params,
-            name="route",
-        )(middle, router, routes)
+            ] + route_scratch + [pltpu.SemaphoreType.DMA((6,))] + remote_sems,
+            compiler_params=remote_params,
+            name="layer",
+        )(images, w_query, w_key, w_value, w_output, router_rows, route_rows, w_in, w_out)
+    middle = attention_over_nodes(images, w_query, w_key, w_value, w_output)[0]
+    middle = jnp.pad(middle, ((0, rows - tokens), (0, 0)))
+    outgoing, gates, places = pl.pallas_call(
+        functools.partial(route_kernel, tokens),
+        out_shape=[blocks] + small,
+        in_specs=[here] * 3,
+        out_specs=[here] * 3,
+        scratch_shapes=route_scratch,
+        compiler_params=params,
+        name="route",
+    )(middle, router_rows, route_rows)
     returned = pl.pallas_call(
         functools.partial(expert_kernel, node_count, columns),
         out_shape=jax.ShapeDtypeStruct((number, CAP, width), jnp.bfloat16),
         in_specs=[here, anywhere, anywhere],
         out_specs=here,
-        scratch_shapes=[
-            pltpu.VMEM((width, hidden_units), jnp.bfloat16),
-            pltpu.VMEM((hidden_units, width), jnp.bfloat16),
-            pltpu.VMEM((number, CAP, width), jnp.bfloat16),
-            pltpu.VMEM((number, CAP, width), jnp.bfloat16),
-            pltpu.VMEM((CHUNK * CAP, width), jnp.float32),
+        scratch_shapes=weight_scratch + [exchange_blocks] * 2 + [
+            total_scratch,
             pltpu.SemaphoreType.DMA((2,)),
-            pltpu.SemaphoreType.DMA((number,)),
-            pltpu.SemaphoreType.DMA((number,)),
-            pltpu.SemaphoreType.DMA((number,)),
-            pltpu.SemaphoreType.DMA((number,)),
-        ],
-        compiler_params=pltpu.CompilerParams(
-            collective_id=0, has_side_effects=True, vmem_limit_bytes=VMEM_BYTES
-        ),
+        ] + remote_sems,
+        compiler_params=remote_params,
         name="experts",
     )(outgoing, w_in, w_out)
-    if node_count > 1:
-        summed = jnp.sum(returned.astype(jnp.float32).reshape(node_count, experts, CAP, width), axis=0)
-        returned = summed.astype(jnp.bfloat16)
+    me = lax.axis_index("node") * columns + lax.axis_index("ep")
+    away = (jnp.arange(number) - me) % number
+    step, ahead = away % (number // PLANES), away // (number // PLANES)
+    returned = jnp.take(returned, step // 2 * CHUNK + (ahead + PLANES - 2) % PLANES * 2 + step % 2, axis=0)
+    summed = jnp.sum(returned.astype(jnp.float32).reshape(node_count, experts, CAP, width), axis=0)
     return pl.pallas_call(
         functools.partial(combine_kernel, tokens),
         out_shape=jax.ShapeDtypeStruct(images.shape, jnp.bfloat16),
@@ -381,7 +472,7 @@
         out_specs=here,
         compiler_params=params,
         name="combine",
-    )(middle, gates, places, returned)
+    )(middle, gates, places, summed.astype(jnp.bfloat16))
 
 
 def solution(mesh):

time: 125 us -> 113 us (0.904)
  Pallas kernels: 122 us -> 110 us
  local copies, waits for them, and re-layouts: 3.26 us -> 1.98 us
    pallas_call x3 -> x1, Pallas kernels: 122 us -> 110 us  [shards(): pl.pallas_call(functools.partial(layer_kernel, tokens, columns), out_shap...]
    unnamed x2 -> x1, local copies, waits for them, and re-layouts: 3.26 us -> 1.98 us
where the time goes in v2:
time: 113 us; the launch traced here: 112 us
  Pallas kernels  110 us (97%)
  local copies, waits for them, and re-layouts  1.98 us (2%)
    pallas_call x1, Pallas kernels, shards(): pl.pallas_call(functools.partial(layer_kernel, tokens, columns), out_shap...  110 us

profile of v2, /device:TPU:1, one launch (start us, length us, event | category | flops | bytes accessed | tf_op | source)
XLA Modules:
  0.0 112.3 jit_solution(15902865090687474906)
XLA Ops:
  0.0 110.3 %layer.1 = bf16[1,257,1280]{2,1,0:T(8,128)(2,1)} custom-call(bf16[1,257,1280]{2,1,0:T(8,128)(2,1)} %images_ref.1, bf16[1280,1280]{1,0:T(8,128)(2,1)} %q_hbm.1, bf16[1280,1280]{1,0:T(8,128)(2,1)} %k_hbm.1, bf16[1280,1280]{1,0:T(8,128)(2,1)} %v_hbm.1, bf16[1280,1280]{1,0:T(8,128)(2,1)} %o_hbm.1, bf16[32,1280]{1,0:T(8,128)(2,1)} %bitcast.4, s32[2,257]{1,0:T(2,128)} %bitcast.5, ...), custom_call_target="tpu_custom_call" | custom-call | tf_op jit(solution)/shard_map/layer/pallas_call | solution.py:420
  110.3 2.0 %copy.11 = bf16[1,257,1280]{2,1,0:T(8,128)(2,1)} copy(bf16[1,257,1280]{2,1,0:T(8,128)(2,1)} %layer.1) | data formatting | bytes 1315840

commit v3 on v2

--- a/solution.py
+++ b/solution.py
@@ -33,49 +33,50 @@
     return jnp.sum(jnp.where(routes[:, which : which + 1] == columns, table, 0.0), axis=1, keepdims=True)
 
 
-def route(tokens, rows, wide, router_ref, routes_ref, middle, out_ref, gate_ref, place_ref, normed, wanted, turned=None):
+def route(tokens, rows, wide, router_ref, routes_ref, middle, gate_ref, place_ref, normed, wanted, turned):
     width = middle.shape[1]
     experts = router_ref.shape[0]
-    slots = experts * CAP
     normed[rows:, :] = jnp.zeros((wide - rows, width), jnp.bfloat16)
     normed[:rows, :] = layer_norm(middle[...]).astype(jnp.bfloat16)
     wanted[...] = jnp.full(wanted.shape, -1.0, jnp.float32)
     wanted[0:2, :tokens] = routes_ref[...].astype(jnp.float32)
     routes_wide = jnp.transpose(wanted[...]).astype(jnp.int32)
-    routes = routes_wide[:rows, :]
     logits = lax.dot_general(
-        normed[:rows, :], router_ref[...], (((1,), (1,)), ((), ())), preferred_element_type=jnp.float32
+        normed[...], router_ref[...], (((1,), (1,)), ((), ())), preferred_element_type=jnp.float32
     )
     columns = lax.broadcasted_iota(jnp.int32, (wide, experts), 1)
     named = jnp.where(routes_wide[:, 0:1] == columns, 1.0, 0.0) + jnp.where(
         routes_wide[:, 1:2] == columns, 1.0, 0.0
     )
     earlier = jnp.where(
-        lax.broadcasted_iota(jnp.int32, (rows, wide), 1) < lax.broadcasted_iota(jnp.int32, (rows, wide), 0),
+        lax.broadcasted_iota(jnp.int32, (wide, wide), 1) < lax.broadcasted_iota(jnp.int32, (wide, wide), 0),
         1.0,
         0.0,
     ).astype(jnp.bfloat16)
     rank = jnp.dot(earlier, named.astype(jnp.bfloat16), preferred_element_type=jnp.float32)
-    slot_of = lax.broadcasted_iota(jnp.int32, (rows, slots), 1)
-    sends = jnp.zeros((rows, slots), jnp.float32)
+    column = lax.broadcasted_iota(jnp.int32, (wide, 8), 1)
+    both = jnp.full((wide, 8), -1.0, jnp.float32)
     for which in range(2):
-        chosen = choose(rows, experts, routes, logits, which)
-        gate_ref[:, which : which + 1] = jax.nn.sigmoid(chosen)
-        turn = choose(rows, experts, routes, rank, which).astype(jnp.int32)
-        place = routes[:, which : which + 1] * CAP + turn
-        kept = place
-        if turned is not None:
-            kept = turned(routes[:, which : which + 1]) * CAP + turn
-        place_ref[:, which : which + 1] = kept
-        sends = sends + jnp.where(place == slot_of, 1.0, 0.0)
-    sends = jnp.concatenate([sends, jnp.zeros((wide - rows, slots), jnp.float32)], axis=0)
-    picks = jnp.transpose(sends).astype(jnp.bfloat16)
-
-    @pl.loop(0, width // TILE)
-    def _(tile):
-        part = pl.ds(pl.multiple_of(tile * TILE, TILE), TILE)
+        route_column = routes_wide[:, which : which + 1]
+        gate_ref[:, which : which + 1] = jax.nn.sigmoid(
+            choose(wide, experts, routes_wide, logits, which)[:rows, :]
+        )
+        turn = choose(wide, experts, routes_wide, rank, which).astype(jnp.int32)
+        place = jnp.where(route_column >= 0, turned(route_column) * CAP + turn, -1)
+        place_ref[:, which : which + 1] = place[:rows, :]
+        both = jnp.where(column == which, place.astype(jnp.float32), both)
+    return jnp.transpose(both).astype(jnp.int32)
+
+
+def gather_rows(across, normed, start, blocks, out_ref, at):
+    wide, width = normed.shape
+    slot_of = lax.broadcasted_iota(jnp.int32, (blocks * CAP, wide), 0) + start
+    picks = jnp.where(across[0:1, :] == slot_of, 1.0, 0.0) + jnp.where(across[1:2, :] == slot_of, 1.0, 0.0)
+    picks = picks.astype(jnp.bfloat16)
+    for tile in range(width // TILE):
+        part = pl.ds(tile * TILE, TILE)
         block = jnp.dot(picks, normed[:, part], preferred_element_type=jnp.float32)
-        out_ref[:, :, part] = block.reshape(experts, CAP, TILE).astype(jnp.bfloat16)
+        out_ref[pl.ds(at, blocks), :, part] = block.reshape(blocks, CAP, TILE).astype(jnp.bfloat16)
 
 
 def attend(tokens, images_ref, loads, weights, middle_ref, inputs, normed, queries, keys, values, mixed):
@@ -89,6 +90,7 @@
     values[rows:, :] = jnp.zeros((wide - rows, width), jnp.bfloat16)
     for at, target in enumerate((queries, keys, values)):
         loads[at].wait()
+        loads[at + 2].start()
 
         @pl.loop(0, width // TILE)
         def _(tile):
@@ -101,12 +103,11 @@
     period = math.lcm(HEAD, LANES)
     valid = lax.broadcasted_iota(jnp.int32, (rows, wide), 1) < tokens
 
-    @pl.loop(0, width // period)
-    def _(turn):
+    for turn in range(width // period):
         for head in range(period // HEAD):
             low = head * HEAD // LANES * LANES
             span = up_to(head * HEAD + HEAD, LANES) - low
-            part = pl.ds(pl.multiple_of(turn * period + low, LANES), span)
+            part = pl.ds(turn * period + low, span)
             lane = lax.broadcasted_iota(jnp.int32, (rows, span), 1) + low
             inside = (lane >= head * HEAD) & (lane < head * HEAD + HEAD)
             query = jnp.where(inside, queries[:, part].astype(jnp.float32), 0.0).astype(jnp.bfloat16)
@@ -115,7 +116,6 @@
             ) * (1.0 / math.sqrt(HEAD))
             scores = jnp.where(valid, scores, -1e30)
             raised = jnp.exp(scores - jnp.max(scores, axis=1, keepdims=True))
-            raised = jnp.where(valid, raised, 0.0)
             probs = (raised * (1.0 / jnp.sum(raised, axis=1, keepdims=True))).astype(jnp.bfloat16)
             result = jnp.dot(probs, values[:, part], preferred_element_type=jnp.float32)
             mixed[:, part] += jnp.where(inside, result, 0.0)
@@ -134,7 +134,14 @@
 
 def route_kernel(tokens, middle_ref, router_ref, routes_ref, out_ref, gate_ref, place_ref, second, wanted):
     rows, wide = middle_ref.shape[0], second.shape[0]
-    route(tokens, rows, wide, router_ref, routes_ref, middle_ref, out_ref, gate_ref, place_ref, second, wanted)
+    across = route(
+        tokens, rows, wide, router_ref, routes_ref, middle_ref, gate_ref, place_ref, second, wanted,
+        lambda expert: expert,
+    )
+
+    @pl.loop(0, out_ref.shape[0] // CHUNK)
+    def _(chunk):
+        gather_rows(across, second, chunk * CHUNK * CAP, CHUNK, out_ref, chunk * CHUNK)
 
 
 def place_of(node_count, columns):
@@ -158,7 +165,7 @@
 
 def exchange(
     node_count, columns, out_ref, loads, back_ref,
-    first, second, arrived, results, total, go_send, go_recv, back_send, back_recv, taken=None,
+    first, second, arrived, results, total, go_send, go_recv, back_send, back_recv, given=None, taken=None,
 ):
     number = node_count * columns
     plane = number // PLANES
@@ -176,7 +183,7 @@
     def go(slot):
         target = (me + offset(slot)) % number
         return pltpu.make_async_remote_copy(
-            src_ref=out_ref.at[target % columns],
+            src_ref=out_ref.at[target % columns if given is None else slot],
             dst_ref=arrived.at[slot],
             send_sem=go_send.at[slot],
             recv_sem=go_recv.at[slot],
@@ -206,13 +213,18 @@
             device_id_type=MESH,
         )
 
-    @pl.loop(0, number)
-    def _(slot):
-        @pl.when(slot != own_slot)
-        def _():
-            go(slot).start()
-
-    arrived[own_slot] = out_ref[me % columns]
+    @pl.loop(0, chunks)
+    def _(chunk):
+        if given is not None:
+            given(chunk)
+        for within in range(CHUNK):
+            slot = chunk * CHUNK + within
+
+            @pl.when(slot != own_slot)
+            def _():
+                go(slot).start()
+
+    arrived[own_slot] = out_ref[me % columns if given is None else own_slot]
     for load in loads:
         load.wait()
     width, hidden_units = first.shape
@@ -287,21 +299,23 @@
         pltpu.make_async_copy(source, first.at[:, pl.ds(at * width, width)], load_sems.at[at])
         for at, source in enumerate((q_hbm, k_hbm, v_hbm, o_hbm))
     ]
-    for load in loads:
+    for load in loads[:2]:
         load.start()
     down = pltpu.make_async_copy(down_hbm.at[0], second, load_sems.at[4])
     up = pltpu.make_async_copy(in_hbm.at[0], first, load_sems.at[5])
-    down.start()
     met = greet(1, columns)
-    attend(tokens, images_ref, loads, first, middle, inputs, normed, queries, keys, values, mixed)
+    attend(tokens, images_ref, loads + [down], first, middle, inputs, normed, queries, keys, values, mixed)
     up.start()
     me = place_of(1, columns)
-    route(
-        tokens, rows, wide, router_ref, routes_ref, middle, outgoing, gates, places, normed_second, wanted,
+    across = route(
+        tokens, rows, wide, router_ref, routes_ref, middle, gates, places, normed_second, wanted,
         lambda expert: slot_for(expert, me, columns),
     )
     met()
     span = CHUNK * CAP
+
+    def given(chunk):
+        gather_rows(across, normed_second, chunk * span, CHUNK, outgoing, chunk * CHUNK)
 
     def taken(chunk):
         column = lax.broadcasted_iota(jnp.int32, (rows, span), 1) + chunk * span
@@ -322,7 +336,7 @@
 
     exchange(
         1, columns, outgoing, [down, up], returned,
-        first, second, arrived, results, total, go_send, go_recv, back_send, back_recv, taken,
+        first, second, arrived, results, total, go_send, go_recv, back_send, back_recv, given, taken,
     )
     result_ref[0] = middle[:tokens, :].astype(jnp.bfloat16)
 

time: 113 us -> 110 us (0.973)
  Pallas kernels: 110 us -> 108 us
    pallas_call x1, Pallas kernels: 110 us -> 108 us  [shards(): pl.pallas_call(functools.partial(layer_kernel, tokens, columns), out_shap...]
where the time goes in v3:
time: 110 us
  Pallas kernels  108 us (98%)
  local copies, waits for them, and re-layouts  1.98 us (2%)
    pallas_call x1, Pallas kernels, shards(): pl.pallas_call(functools.partial(layer_kernel, tokens, columns), out_shap...  108 us

profile of v3, /device:TPU:1, one launch (start us, length us, event | category | flops | bytes accessed | tf_op | source)
XLA Modules:
  0.0 110.1 jit_solution(4292796782460352811)
XLA Ops:
  0.0 108.1 %layer.1 = bf16[1,257,1280]{2,1,0:T(8,128)(2,1)} custom-call(bf16[1,257,1280]{2,1,0:T(8,128)(2,1)} %images_ref.1, bf16[1280,1280]{1,0:T(8,128)(2,1)} %q_hbm.1, bf16[1280,1280]{1,0:T(8,128)(2,1)} %k_hbm.1, bf16[1280,1280]{1,0:T(8,128)(2,1)} %v_hbm.1, bf16[1280,1280]{1,0:T(8,128)(2,1)} %o_hbm.1, bf16[32,1280]{1,0:T(8,128)(2,1)} %bitcast.4, s32[2,257]{1,0:T(2,128)} %bitcast.5, ...), custom_call_target="tpu_custom_call" | custom-call | tf_op jit(solution)/shard_map/layer/pallas_call | solution.py:434
  108.1 2.0 %copy.11 = bf16[1,257,1280]{2,1,0:T(8,128)(2,1)} copy(bf16[1,257,1280]{2,1,0:T(8,128)(2,1)} %layer.1) | data formatting | bytes 1315840
